TPU v7x, 32 devices: a whole 2x2x4 slice. The times are simulated.
32 devices in a mesh: seq: 16 (over z, y, x), head: 2 (over core).
Axes of the slice: x: 2, y: 2, z: 4, core: 2. Of those that a mesh axis runs over, the one named last changes fastest.
Arguments:
- queries: bfloat16 [6144, 8192], P('seq', 'head'), may hold values from -6 to 6
- keys: bfloat16 [6144, 8192], P('seq', 'head'), may hold values from -6 to 6
- values: bfloat16 [6144, 8192], P('seq', 'head'), may hold values from -6 to 6
- norm_gain: float32 [8192], P('head'), may hold values from 0.25 to 1.75
- out_weight: bfloat16 [8192, 6144], P(None, 'head'), may hold values from -0.0625 to 0.0625
Outputs:
- layer_out: bfloat16 [6144, 6144], P('seq', 'head')
All inputs are finite; a program needn't handle non-finite values.
Results may differ from a plain program's by a relative error of at most 0.0058.
Values may be sent and summed in bfloat16 or wider, within the bound.
A program may use at most 192 MiB of HBM per device.

v0:
```python
import jax
import jax.numpy as jnp
from jax import lax
from jax.sharding import PartitionSpec as P

HEAD_DIM = 128


def entering(value, axis, join, neutral):
    count, mine = (lax.axis_size(axis), lax.axis_index(axis))
    pieces = lax.all_gather(value, axis)
    so_far = jnp.full_like(value, 0) + jnp.asarray(neutral, value.dtype)

    def hop(position, so_far):
        longer = join(so_far, pieces[position])
        return jnp.where(position < mine, longer, so_far)

    return lax.fori_loop(0, count - 1, hop, so_far)


def shards(queries, keys, values, norm_gain, out_weight):
    rows, width = queries.shape
    heads = width // HEAD_DIM
    qa = (
        jax.nn.silu(queries.astype(jnp.float32)).astype(jnp.bfloat16).reshape(rows, heads, HEAD_DIM)
    )
    ka = jax.nn.silu(keys.astype(jnp.float32)).astype(jnp.bfloat16).reshape(rows, heads, HEAD_DIM)
    vv = values.reshape(rows, heads, HEAD_DIM)
    state = jnp.einsum("thd,the->hde", ka, vv, preferred_element_type=jnp.float32)

    def combine(earlier, later):
        return earlier + later

    prefix = entering(state, "seq", combine, jnp.zeros_like(state))
    inter = jnp.einsum(
        "thd,hde->the", qa.astype(jnp.float32), prefix, precision=lax.Precision.HIGHEST
    )
    causal = jnp.arange(rows)[:, None] >= jnp.arange(rows)[None, :]
    scores = jnp.einsum("thd,shd->hts", qa, ka, preferred_element_type=jnp.float32)
    scores = jnp.where(causal[None], scores, 0.0).astype(jnp.bfloat16)
    intra = jnp.einsum("hts,she->the", scores, vv, preferred_element_type=jnp.float32)
    attn = inter + intra
    mean_sq = jnp.mean(attn * attn, axis=-1, keepdims=True)
    gain = norm_gain.reshape(heads, HEAD_DIM)
    normed = (
        (attn * lax.rsqrt(mean_sq + 1e-06) * gain[None]).astype(jnp.bfloat16).reshape(rows, width)
    )
    total = jnp.dot(
        lax.all_gather(normed, "head", axis=1, tiled=True),
        out_weight,
        preferred_element_type=jnp.float32,
    )
    return total.astype(jnp.bfloat16)


def solution(mesh):
    in_specs = (P("seq", "head"), P("seq", "head"), P("seq", "head"), P("head"), P(None, "head"))
    out_specs = P("seq", "head")
    return jax.shard_map(shards, mesh=mesh, in_specs=in_specs, out_specs=out_specs, check_vma=False)
```

profile of v0, /device:TPU:0, one launch (start us, length us, event | category | flops | bytes accessed | tf_op | source)
XLA Modules:
  0.0 488.5 jit_solution(14199027927535599769)
XLA Ops:
  6.5 0.0 all-gather.6.cloned.1.call-start
  6.5 3.7 fusion.6
  10.2 2.8 copy.17
  13.0 0.0 copy-start
  13.0 4.8 copy.18
  17.8 0.0 copy-done
  17.8 4.6 fusion.24
  22.4 0.0 all-gather.6.cloned.1.call-update
  22.5 0.2 all-gather.4.cloned.1.call-start
  22.8 353.4 %all-gather.6.cloned.1.call-done = f32[512,128,128]{2,1,0:T(8,128)} async-done(((f32[32,128,128]{2,1,0:T(8,128)}), f32[512,128,128]{2,1,0:T(8,128)}) %all-gather.6.cloned.1.call-update) | async-done | bytes 33554448 | tf_op jit(solution)/shard_map/all_gather | solution.py:11
  376.2 35.0 %while.14 = (s32[]{:T(128)}, f32[32,128,128]{2,1,0:T(8,128)S(1)}, s32[]{:T(128)}, f32[16,32,128,128]{3,2,1,0:T(8,128)}, s32[]{:T(128)}, /*index=5*/s32[]{:T(128)}) while((s32[]{:T(128)}, f32[32,128,128]{2,1,0:T(8,128)S(1)}, s32[]{:T(128)}, f32[16,32,128,128]{3,2,1,0:T(8,128)}, s32[]{:T(128)}, /*index=5*/s32[]{:T(128)}) %tuple.40), condition=%wide.region_1.2_spmd.clone, body=%wide.region_0.1_spmd.clone.sunk | while | flops 1572868 | bytes 6291549 | solution.py:18
  376.2 2.3 add_select_fusion.2
  378.5 2.3 add_select_fusion.2
  380.8 2.3 add_select_fusion.2
  383.2 2.3 add_select_fusion.2
  385.5 2.3 add_select_fusion.2
  387.9 2.3 add_select_fusion.2
  390.2 2.3 add_select_fusion.2
  392.5 2.3 add_select_fusion.2
  394.9 2.3 add_select_fusion.2
  397.2 2.3 add_select_fusion.2
  399.5 2.3 add_select_fusion.2
  401.9 2.3 add_select_fusion.2
  404.2 2.3 add_select_fusion.2
  406.5 2.3 add_select_fusion.2
  408.9 2.3 add_select_fusion.2
  411.2 9.3 %fusion.16 = f32[32,128,384]{2,1,0:T(8,128)} fusion(f32[32,128,128]{2,1,0:T(8,128)S(1)} %get-tuple-element.84, bf16[384,4096]{1,0:T(8,128)(2,1)} %param.7), kind=kOutput, calls=%fused_computation.24 | convolution fusion | flops 2425356288 | bytes 11534336 | tf_op jit(solution)/shard_map/thd,hde->the/dot_general | solution.py:35
  420.5 0.0 copy-start.1
  420.5 10.7 %multiply_reduce_fusion = (f32[384,32]{0,1:T(8,128)S(1)}, f32[32,384,128]{1,2,0:T(8,128)}) fusion(f32[32,128,384]{2,1,0:T(8,128)} %fusion.16, bf16[384,32,128]{0,2,1:T(8,128)(2,1)} %bitcast.46, pred[384,384]{1,0:T(8,128)(4,1)S(1)} %iota_compare_fusion, bf16[384,32,128]{0,2,1:T(8,128)(2,1)} %bitcast.43, bf16[384,4096]{1,0:T(8,128)(2,1)} %param.7), kind=kOutput, calls=%fused_computation.19 | convolution fusion | flops 2439499776 | bytes 22216704 | tf_op jit(solution)/shard_map/hts,she->the/dot_general | solution.py:41
  431.2 0.0 copy-done.1
  431.2 6.9 %multiply_convert_fusion = bf16[384,32,128]{0,2,1:T(8,128)(2,1)} fusion(f32[32,128]{1,0:T(8,128)S(1)} %bitcast.49, f32[384,32]{0,1:T(8,128)S(1)} %add_rsqrt_fusion, f32[32,384,128]{1,2,0:T(8,128)} %get-tuple-element.109, f32[32,128,384]{2,1,0:T(8,128)} %fusion.16), kind=kLoop, calls=%fused_computation.18 | loop fusion | flops 6291456 | bytes 15794176 | tf_op jit(solution)/shard_map/convert_element_type | solution.py:46
  438.1 0.0 all-gather.4.cloned.1.call-update
  438.1 15.1 %all-gather.4.cloned.1.call-done = bf16[384,8192]{0,1:T(8,128)(2,1)} async-done(((bf16[384,4096]{0,1:T(8,128)(2,1)}), bf16[384,8192]{0,1:T(8,128)(2,1)}) %all-gather.4.cloned.1.call-update) | async-done | bytes 6291472 | tf_op jit(solution)/shard_map/all_gather | solution.py:49
  453.2 28.5 %convolution_convert_fusion = bf16[384,3072]{1,0:T(8,128)(2,1)} fusion(bf16[384,8192]{0,1:T(8,128)(2,1)} %all-gather.4.cloned.1.call-done, bf16[8192,3072]{1,0:T(8,128)(2,1)} %param.11), kind=kOutput, calls=%fused_computation.21 | convolution fusion | flops 19328532480 | bytes 58982400 | tf_op jit(solution)/shard_map/dot_general | solution.py:48
  (3 shorter events, 0.1 us)
Async XLA Ops:
  6.5 369.6 %all-gather.6.cloned.1.call-start = ((), (), s32[]{:S(2)}) async-start(), calls=%async_computation.1 | async-start | bytes 35651584 | tf_op jit(solution)/shard_map/all_gather | solution.py:11
  13.0 4.8 copy-start
  22.5 430.8 %all-gather.4.cloned.1.call-start = ((), (), s32[]{:S(2)}) async-start(), calls=%async_computation | async-start | bytes 9437184 | tf_op jit(solution)/shard_map/all_gather | solution.py:49
  420.5 10.7 %copy-start.1 = (f32[4096]{0:T(1024)S(1)}, f32[4096]{0:T(1024)}, u32[]{:S(2)}) copy-start(f32[4096]{0:T(1024)} %param.10) | copy-start | bytes 49156
Sparse Core Ops, SparseCore 0:
  22.6 353.5 all-gather.5
  438.3 14.9 all-gather.3
where the time goes:
time: 489 us
  waiting for transfers between devices  369 us (75%)
  matrix products  53.1 us (11%)
  other arithmetic  45.3 us (9%)
  between operations  13.5 us (3%)
  local copies, waits for them, and re-layouts  7.6 us (2%)
    all_gather x1, waiting for transfers between devices, entering(): pieces = lax.all_gather(value, axis)  353 us
    select_n x15, other arithmetic, hop(): return jnp.where(position < mine, longer, so_far)  34.7 us
    dot_general x1, matrix products, shards(): jnp.dot(lax.all_gather(normed, 'head', axis=1, tiled=True), out_weight, p...  28.5 us
    all_gather x1, waiting for transfers between devices, shards(): lax.all_gather(normed, 'head', axis=1, tiled=True)  15.1 us
    dot_general x1, matrix products, shards(): jnp.einsum('hts,she->the', scores, vv, preferred_element_type=jnp.float32)  10.7 us
  transfers between devices with their start and end apart: 2, of which 2 were waited for; matrix products, arithmetic and copies ran while one was open for 0% of the time, Pallas kernels for 0%

commit v1 on v0

v1 whole, which is shorter than its diff:
```python
import functools

import jax
import jax.numpy as jnp
from jax import lax
from jax.experimental import pallas as pl
from jax.experimental.pallas import tpu as pltpu
from jax.sharding import PartitionSpec as P

HEAD_DIM = 128
MEMBERS = 4
MESH = pl.DeviceIdType.MESH
F32, BF16 = jnp.float32, jnp.bfloat16


def silu(x):
    half = 0.5 * x.astype(F32)
    return (half * (1.0 + jnp.tanh(half))).astype(BF16)


def loop(count, body):
    def step(i, carry):
        body(i)
        return carry

    lax.fori_loop(0, count, step, 0)


def kernel(
    n, m, q_hbm, k_hbm, v_hbm, gain_ref, w_hbm, out_hbm,
    qb, kb, vb, intra, stage, held, chain_in, chain_out, ret_out, ret_in, normed, acc, outb, wb,
    load_sem, w_sem, s1_send, s1_recv, ch_send, ch_recv, rt_send, rt_recv, hd_send, hd_recv, out_sem,
):
    parts, members, rows, width = qb.shape
    per = width // HEAD_DIM
    groups = n // members
    slots = wb.shape[0]
    columns = acc.shape[1]
    tile = 512 if columns % 512 == 0 else columns
    tiles = columns // tile
    own_heads = parts * per
    local = members * own_heads

    seq, head = lax.axis_index("seq"), lax.axis_index("head")
    group, member = lax.div(seq, members), lax.rem(seq, members)

    def mate(d):
        return lax.rem(member + d, members)

    def seq_of(i):
        return {"seq": group * members + i}

    def load(which, hbm, buf, p, j):
        at = pl.multiple_of((j * own_heads + p * per) * HEAD_DIM, HEAD_DIM)
        return pltpu.make_async_copy(
            hbm.at[:, pl.ds(at, width)], buf.at[p, j], load_sem.at[which, p, j]
        )

    def weights(s, j):
        p, r = lax.div(s, m), lax.rem(s, m)
        source = lax.rem(head + r, m)
        at = pl.multiple_of((source * local + j * own_heads + p * per) * HEAD_DIM, HEAD_DIM)
        slot = lax.rem(s, slots)
        return pltpu.make_async_copy(
            w_hbm.at[pl.ds(at, width), :], wb.at[slot, pl.ds(j * width, width), :], w_sem.at[slot, j]
        )

    def to_owner(p, j):
        return pltpu.make_async_remote_copy(
            src_ref=stage.at[p, j], dst_ref=held.at[p, member],
            send_sem=s1_send.at[p, j], recv_sem=s1_recv.at[p, member],
            device_id=seq_of(j), device_id_type=MESH,
        )

    def from_mate(p, i):
        return pltpu.make_async_remote_copy(
            src_ref=stage.at[p, i], dst_ref=held.at[p, i],
            send_sem=s1_send.at[p, i], recv_sem=s1_recv.at[p, i],
            device_id=seq_of(i), device_id_type=MESH,
        )

    def chain(p):
        return pltpu.make_async_remote_copy(
            src_ref=chain_out.at[p], dst_ref=chain_in.at[p],
            send_sem=ch_send.at[p], recv_sem=ch_recv.at[p],
            device_id={"seq": lax.rem(seq + members, n)}, device_id_type=MESH,
        )

    def give_back(p, i):
        return pltpu.make_async_remote_copy(
            src_ref=ret_out.at[p, i], dst_ref=ret_in.at[p, member],
            send_sem=rt_send.at[p, i], recv_sem=rt_recv.at[p, member],
            device_id=seq_of(i), device_id_type=MESH,
        )

    def get_back(p, j):
        return pltpu.make_async_remote_copy(
            src_ref=ret_out.at[p, j], dst_ref=ret_in.at[p, j],
            send_sem=rt_send.at[p, j], recv_sem=rt_recv.at[p, j],
            device_id=seq_of(j), device_id_type=MESH,
        )

    def to_head(p, r):
        return pltpu.make_async_remote_copy(
            src_ref=normed.at[p, 0], dst_ref=normed.at[p, m - r],
            send_sem=hd_send.at[p, r], recv_sem=hd_recv.at[p, m - r],
            device_id={"head": lax.rem(head + r, m)}, device_id_type=MESH,
        )

    def from_head(p, r):
        return pltpu.make_async_remote_copy(
            src_ref=normed.at[p, 0], dst_ref=normed.at[p, r],
            send_sem=hd_send.at[p, r], recv_sem=hd_recv.at[p, r],
            device_id={"head": lax.rem(head + r, m)}, device_id_type=MESH,
        )

    def write(t):
        cols = pl.ds(pl.multiple_of(t * tile, tile), tile)
        return pltpu.make_async_copy(outb.at[:, cols], out_hbm.at[:, cols], out_sem.at[t])

    def start_loads(p):
        def both(j):
            load(0, k_hbm, kb, p, j).start()
            load(1, v_hbm, vb, p, j).start()

        loop(members, both)

    loop(parts, start_loads)
    loop(parts, lambda p: loop(members, lambda j: load(2, q_hbm, qb, p, j).start()))
    loop(slots, lambda s: loop(members, lambda j: weights(s, j).start()))

    barrier = pltpu.get_barrier_semaphore()
    for d in range(1, members):
        pl.semaphore_signal(barrier, inc=1, device_id=seq_of(mate(d)), device_id_type=MESH)
    for r in range(1, m):
        pl.semaphore_signal(
            barrier, inc=1, device_id={"head": lax.rem(head + r, m)}, device_id_type=MESH
        )

    @pl.when(group > 0)
    def _():
        pl.semaphore_signal(
            barrier, inc=1, device_id={"seq": lax.rem(seq - members + n, n)}, device_id_type=MESH
        )

    @pl.when(group < groups - 1)
    def _():
        pl.semaphore_signal(
            barrier, inc=1, device_id={"seq": lax.rem(seq + members, n)}, device_id_type=MESH
        )

    beside = jnp.where(group > 0, 1, 0) + jnp.where(group < groups - 1, 1, 0)
    pl.semaphore_wait(barrier, members - 1 + m - 1 + beside)

    def states(p):
        def one(d):
            j = mate(d + 1)
            load(0, k_hbm, kb, p, j).wait()
            load(1, v_hbm, vb, p, j).wait()
            ka = silu(kb[p, j])
            kb[p, j] = ka
            both = lax.dot_general(
                ka, vb[p, j], (((0,), (0,)), ((), ())), preferred_element_type=F32
            )
            diagonal = [
                both[c * HEAD_DIM : (c + 1) * HEAD_DIM, c * HEAD_DIM : (c + 1) * HEAD_DIM].astype(BF16)
                for c in range(per)
            ]

            @pl.when(j != member)
            def _():
                for c in range(per):
                    stage[p, j, c] = diagonal[c]
                to_owner(p, j).start()

            @pl.when(j == member)
            def _():
                for c in range(per):
                    held[p, member, c] = diagonal[c]

        loop(members, one)

    def combine(p):
        for d in range(1, members):
            from_mate(p, mate(d)).wait_recv()

        @pl.when(group > 0)
        def _():
            chain(p).wait_recv()

        @pl.when(group == 0)
        def _():
            chain_in[p] = jnp.zeros(chain_in.shape[1:], F32)

        @pl.when(group < groups - 1)
        def _():
            total = chain_in[p]
            for i in range(members):
                total = total + held[p, i].astype(F32)
            chain_out[p] = total
            chain(p).start()

        before = chain_in[p]
        for i in range(members):
            rounded = before.astype(BF16)

            @pl.when(member != i)
            def _():
                ret_out[p, i] = rounded
                give_back(p, i).start()

            @pl.when(member == i)
            def _():
                ret_in[p, i] = rounded

            if i < members - 1:
                before = before + held[p, i].astype(F32)

    block = 128 if rows % 128 == 0 else rows

    def inside(p):
        at_or_before = (
            lax.broadcasted_iota(jnp.int32, (block, block), 0)
            >= lax.broadcasted_iota(jnp.int32, (block, block), 1)
        )

        def one(j):
            load(2, q_hbm, qb, p, j).wait()
            qb[p, j] = silu(qb[p, j])
            for c in range(per):
                lanes = slice(c * HEAD_DIM, (c + 1) * HEAD_DIM)
                for b in range(rows // block):
                    tokens = slice(b * block, (b + 1) * block)
                    upto = slice(0, (b + 1) * block)
                    qa = qb[p, j, tokens, lanes]
                    scores = lax.dot_general(
                        qa, kb[p, j, upto, lanes], (((1,), (1,)), ((), ())),
                        preferred_element_type=F32,
                    )
                    last = jnp.where(at_or_before, scores[:, b * block :], 0.0).astype(BF16)
                    if b:
                        last = jnp.concatenate(
                            [scores[:, : b * block].astype(BF16), last], axis=1
                        )
                    intra[p, j, tokens, lanes] = jnp.dot(
                        last, vb[p, j, upto, lanes], preferred_element_type=F32
                    )

        loop(members, one)

    def project(s, a):
        slot = lax.rem(s, slots)
        loop(members, lambda j: weights(s, j).wait())

        def one(t):
            cols = pl.ds(pl.multiple_of(t * tile, tile), tile)
            acc[:, cols] += jnp.dot(a[...], wb[slot, :, cols], preferred_element_type=F32)

        loop(tiles, one)

        @pl.when(s + slots < parts * m)
        def _():
            loop(members, lambda j: weights(s + slots, j).start())

    def finish(p):
        for d in range(1, members):
            get_back(p, mate(d)).wait_recv()

        def one(j):
            for c in range(per):
                lanes = slice(c * HEAD_DIM, (c + 1) * HEAD_DIM)
                inter = jnp.dot(qb[p, j, :, lanes], ret_in[p, j, c], preferred_element_type=F32)
                attn = inter + intra[p, j, :, lanes]
                mean_sq = jnp.mean(attn * attn, axis=-1, keepdims=True)
                value = attn * lax.rsqrt(mean_sq + 1e-06) * gain_ref[j, p, :, lanes]
                at = pl.multiple_of(j * width + c * HEAD_DIM, HEAD_DIM)
                normed[p, 0, :, pl.ds(at, HEAD_DIM)] = value.astype(BF16)

        loop(members, one)
        loop(m - 1, lambda r: to_head(p, r + 1).start())
        project(p * m, normed.at[p, 0])

        def other(r):
            from_head(p, r + 1).wait_recv()
            project(p * m + r + 1, normed.at[p, r + 1])

        loop(m - 1, other)

    loop(parts, states)
    acc[...] = jnp.zeros(acc.shape, F32)

    def slot_step(t):
        u = t - group

        @pl.when((u >= 0) & (u < parts))
        def _():
            combine(u)

        @pl.when(t < parts)
        def _():
            inside(t)

        @pl.when(t >= groups)
        def _():
            finish(t - groups)

    loop(parts + groups, slot_step)

    def emit(t):
        cols = pl.ds(pl.multiple_of(t * tile, tile), tile)
        outb[:, cols] = acc[:, cols].astype(BF16)
        write(t).start()

    loop(tiles, emit)

    def sent(p):
        for d in range(1, members):
            to_owner(p, mate(d)).wait_send()
            give_back(p, mate(d)).wait_send()

        @pl.when(group < groups - 1)
        def _():
            chain(p).wait_send()

        loop(m - 1, lambda r: to_head(p, r + 1).wait_send())

    loop(parts, sent)
    loop(tiles, lambda t: write(t).wait())


def shards(n, m, queries, keys, values, norm_gain, out_weight):
    rows, wide = queries.shape
    columns = out_weight.shape[1]
    heads = wide // HEAD_DIM
    own = heads // MEMBERS
    per = 2 if own % 2 == 0 else 1
    parts = own // per
    width = per * HEAD_DIM
    slots = min(4, parts * m)
    tile = 512 if columns % 512 == 0 else columns
    gain = norm_gain.reshape(MEMBERS, parts, 1, width)
    square = (per, HEAD_DIM, HEAD_DIM)
    grid = (parts, MEMBERS)
    dma = pltpu.SemaphoreType.DMA
    anywhere = pl.BlockSpec(memory_space=pl.ANY)
    return pl.pallas_call(
        functools.partial(kernel, n, m),
        out_shape=jax.ShapeDtypeStruct((rows, columns), BF16),
        in_specs=[anywhere] * 3 + [pl.BlockSpec(memory_space=pltpu.VMEM), anywhere],
        out_specs=anywhere,
        scratch_shapes=[
            pltpu.VMEM(grid + (rows, width), BF16),
            pltpu.VMEM(grid + (rows, width), BF16),
            pltpu.VMEM(grid + (rows, width), BF16),
            pltpu.VMEM(grid + (rows, width), F32),
            pltpu.VMEM(grid + square, BF16),
            pltpu.VMEM(grid + square, BF16),
            pltpu.VMEM((parts,) + square, F32),
            pltpu.VMEM((parts,) + square, F32),
            pltpu.VMEM(grid + square, BF16),
            pltpu.VMEM(grid + square, BF16),
            pltpu.VMEM((parts, m, rows, MEMBERS * width), BF16),
            pltpu.VMEM((rows, columns), F32),
            pltpu.VMEM((rows, columns), BF16),
            pltpu.VMEM((slots, MEMBERS * width, columns), BF16),
            dma((3,) + grid),
            dma((slots, MEMBERS)),
            dma(grid), dma(grid),
            dma((parts,)), dma((parts,)),
            dma(grid), dma(grid),
            dma((parts, m)), dma((parts, m)),
            dma((columns // tile,)),
        ],
        compiler_params=pltpu.CompilerParams(
            collective_id=0, has_side_effects=True, vmem_limit_bytes=63 * 1024 * 1024
        ),
        cost_estimate=pl.CostEstimate(
            flops=2 * rows * wide * m * columns, bytes_accessed=2 * wide * m * columns,
            transcendentals=2 * rows * wide,
        ),
    )(queries, keys, values, gain, out_weight)


def solution(mesh):
    n, m = mesh.shape["seq"], mesh.shape["head"]
    in_specs = (P("seq", "head"), P("seq", "head"), P("seq", "head"), P("head"), P(None, "head"))
    return jax.shard_map(
        functools.partial(shards, n, m), mesh=mesh, in_specs=in_specs,
        out_specs=P("seq", "head"), check_vma=False,
    )
```

time: 489 us -> 69.3 us (0.14)
  waiting for transfers between devices: 369 us -> 0 us
  Pallas kernels: 0 us -> 65.9 us
  matrix products: 53.1 us -> 0 us
  other arithmetic: 45.3 us -> 0 us
  between operations: 13.5 us -> 0.01 us
    all_gather x2 -> x0, waiting for transfers between devices: 369 us -> none  [the longest x1 353 us: entering(): pieces = lax.all_gather(value, axis)]
    pallas_call x0 -> x1, Pallas kernels: none -> 65.9 us  [shards(): pl.pallas_call(functools.partial(kernel, n, m), out_shape=jax.ShapeDtypeS...]
    dot_general x4 -> x0, matrix products: 53.1 us -> none  [the longest x1 28.5 us: shards(): jnp.dot(lax.all_gather(normed, 'head', axis=1, tiled=True), out_weight, p...]
    select_n x15 -> x0, other arithmetic: 34.7 us -> none  [hop(): return jnp.where(position < mine, longer, so_far)]
    convert_element_type x2 -> x0, other arithmetic: 10.6 us -> none  [the longest x1 6.91 us: shards(): (attn * lax.rsqrt(mean_sq + 1e-06) * gain[None]).astype(jnp.bfloat16)]
    reshape x2 -> x0, local copies, waits for them, and re-layouts: 7.59 us -> none  [the longest x1 4.8 us: shards(): vv = values.reshape(rows, heads, HEAD_DIM)]
  transfers between devices with their start and end apart: 2 -> 0, of which waited for: 2 -> 0; matrix products, arithmetic and copies ran while one was open for 0% -> 0% of each run, Pallas kernels for 0% -> 0%
where the time goes in v1:
time: 69.3 us; the launch traced here: 69.1 us
  Pallas kernels  65.9 us (95%)
  local copies, waits for them, and re-layouts  3.22 us (5%)
    pallas_call x1, Pallas kernels, shards(): pl.pallas_call(functools.partial(kernel, n, m), out_shape=jax.ShapeDtypeS...  65.9 us
    unnamed x1, local copies, waits for them, and re-layouts  3.22 us

profile of v1, /device:TPU:0, one launch (start us, length us, event | category | flops | bytes accessed | tf_op | source)
XLA Modules:
  0.0 69.1 jit_solution(3477053798157732343)
XLA Ops:
  0.0 65.9 %shard_map.55 = bf16[384,3072]{1,0:T(8,128)(2,1)} custom-call(bf16[384,4096]{1,0:T(8,128)(2,1)} %q_hbm.1, bf16[384,4096]{1,0:T(8,128)(2,1)} %k_hbm.1, bf16[384,4096]{1,0:T(8,128)(2,1)} %v_hbm.1, f32[4,4,1,256]{3,2,1,0:T(1,128)} %bitcast.1, bf16[8192,3072]{1,0:T(8,128)(2,1)} %w_hbm.1), custom_call_target="tpu_custom_call" | custom-call | flops 19327352832 | bytes 50331648 | tf_op jit(solution)/shard_map/pallas_call | solution.py:346
  65.9 3.2 %copy.7 = bf16[384,3072]{1,0:T(8,128)(2,1)} copy(bf16[384,3072]{1,0:T(8,128)(2,1)} %shard_map.55) | data formatting | bytes 4718592

commit v2 on v1

--- a/solution.py
+++ b/solution.py
@@ -18,12 +18,12 @@
     return (half * (1.0 + jnp.tanh(half))).astype(BF16)
 
 
-def loop(count, body):
+def loop(count, body, unroll=False):
     def step(i, carry):
         body(i)
         return carry
 
-    lax.fori_loop(0, count, step, 0)
+    lax.fori_loop(0, count, step, 0, unroll=unroll)
 
 
 def kernel(
@@ -36,7 +36,7 @@
     groups = n // members
     slots = wb.shape[0]
     columns = acc.shape[1]
-    tile = 512 if columns % 512 == 0 else columns
+    tile = 1536 if columns % 1536 == 0 else columns
     tiles = columns // tile
     own_heads = parts * per
     local = members * own_heads
@@ -216,7 +216,7 @@
             if i < members - 1:
                 before = before + held[p, i].astype(F32)
 
-    block = 128 if rows % 128 == 0 else rows
+    block = rows
 
     def inside(p):
         at_or_before = (
@@ -226,27 +226,20 @@
 
         def one(j):
             load(2, q_hbm, qb, p, j).wait()
-            qb[p, j] = silu(qb[p, j])
+            qa = silu(qb[p, j])
+            qb[p, j] = qa
             for c in range(per):
                 lanes = slice(c * HEAD_DIM, (c + 1) * HEAD_DIM)
-                for b in range(rows // block):
-                    tokens = slice(b * block, (b + 1) * block)
-                    upto = slice(0, (b + 1) * block)
-                    qa = qb[p, j, tokens, lanes]
-                    scores = lax.dot_general(
-                        qa, kb[p, j, upto, lanes], (((1,), (1,)), ((), ())),
-                        preferred_element_type=F32,
-                    )
-                    last = jnp.where(at_or_before, scores[:, b * block :], 0.0).astype(BF16)
-                    if b:
-                        last = jnp.concatenate(
-                            [scores[:, : b * block].astype(BF16), last], axis=1
-                        )
-                    intra[p, j, tokens, lanes] = jnp.dot(
-                        last, vb[p, j, upto, lanes], preferred_element_type=F32
-                    )
-
-        loop(members, one)
+                scores = lax.dot_general(
+                    qa[:, lanes], kb[p, j, :, lanes], (((1,), (1,)), ((), ())),
+                    preferred_element_type=F32,
+                )
+                scores = jnp.where(at_or_before, scores, 0.0).astype(BF16)
+                intra[p, j, :, lanes] = jnp.dot(
+                    scores, vb[p, j, :, lanes], preferred_element_type=F32
+                )
+
+        loop(members, one, True)
 
     def project(s, a):
         slot = lax.rem(s, slots)
@@ -276,7 +269,7 @@
                 at = pl.multiple_of(j * width + c * HEAD_DIM, HEAD_DIM)
                 normed[p, 0, :, pl.ds(at, HEAD_DIM)] = value.astype(BF16)
 
-        loop(members, one)
+        loop(members, one, True)
         loop(m - 1, lambda r: to_head(p, r + 1).start())
         project(p * m, normed.at[p, 0])
 
@@ -337,7 +330,7 @@
     parts = own // per
     width = per * HEAD_DIM
     slots = min(4, parts * m)
-    tile = 512 if columns % 512 == 0 else columns
+    tile = 1536 if columns % 1536 == 0 else columns
     gain = norm_gain.reshape(MEMBERS, parts, 1, width)
     square = (per, HEAD_DIM, HEAD_DIM)
     grid = (parts, MEMBERS)

time: 69.3 us -> 59.3 us (0.86)
  the two profiles are of different devices: /device:TPU:0 before, /device:TPU:24 now
where the time goes in v2:
time: 59.3 us; the launch traced here: 59.1 us
  Pallas kernels  55.9 us (94%)
  local copies, waits for them, and re-layouts  3.22 us (5%)
    pallas_call x1, Pallas kernels, shards(): pl.pallas_call(functools.partial(kernel, n, m), out_shape=jax.ShapeDtypeS...  55.9 us
    unnamed x1, local copies, waits for them, and re-layouts  3.22 us

profile of v2, /device:TPU:24, one launch (start us, length us, event | category | flops | bytes accessed | tf_op | source)
XLA Modules:
  0.0 59.1 jit_solution(13047048697256411781)
XLA Ops:
  0.0 55.9 %shard_map.55 = bf16[384,3072]{1,0:T(8,128)(2,1)} custom-call(bf16[384,4096]{1,0:T(8,128)(2,1)} %q_hbm.1, bf16[384,4096]{1,0:T(8,128)(2,1)} %k_hbm.1, bf16[384,4096]{1,0:T(8,128)(2,1)} %v_hbm.1, f32[4,4,1,256]{3,2,1,0:T(1,128)} %bitcast.1, bf16[8192,3072]{1,0:T(8,128)(2,1)} %w_hbm.1), custom_call_target="tpu_custom_call" | custom-call | flops 19327352832 | bytes 50331648 | tf_op jit(solution)/shard_map/pallas_call | solution.py:339
  55.9 3.2 %copy.7 = bf16[384,3072]{1,0:T(8,128)(2,1)} copy(bf16[384,3072]{1,0:T(8,128)(2,1)} %shard_map.55) | data formatting | bytes 4718592
